TPU v7x, 32 devices: a whole 2x2x4 slice. The times are simulated.
32 devices in a mesh: sweep: 4 (over x, core), nd: 8 (over z, y).
Axes of the slice: x: 2, y: 2, z: 4, core: 2. Of those that a mesh axis runs over, the one named last changes fastest.
Arguments:
- f_int: float32 [4, 4, 262144], P('sweep', None, 'nd'), may hold values from -6 to 6
- f_sep: float32 [4, 4, 8192], P('sweep', None, 'nd'), may hold values from -6 to 6
- leaf_inverse: bfloat16 [4, 2048, 128, 128], P('sweep', 'nd'), may hold values from -6 to 6
- sep_inverse: bfloat16 [4, 64, 128, 128], P('sweep', 'nd'), may hold values from -6 to 6
- sep_map: int32 [4, 16384], P('sweep', 'nd'), may hold values from 0 to 8191
- couple: float32 [4, 16384], P('sweep', 'nd'), may hold values from 0.5 to 1.4
- trace_coef: float32 [4, 16384], P('sweep', 'nd'), may hold values from 0.5 to 1
Outputs:
- x_int: float32 [4, 4, 262144], P('sweep', None, 'nd')
- x_sep: float32 [4, 4, 8192], P('sweep', None, 'nd')
All inputs are finite; a program needn't handle non-finite values.
Results may differ from a plain program's by a relative error of at most 0.0051.
Values sent between devices are 32-bit elements; how exact they have to be, the bound alone decides.
A program may use at most 128 MiB of HBM per device.

v0:
```python
import jax
import jax.numpy as jnp
from jax import lax
from jax.sharding import PartitionSpec as P

PLANES = 16
EDGE = 128


def passed_along(array, axis, by):
    devices = lax.axis_size(axis)
    pairs = [(i, i + by) for i in range(devices) if 0 <= i + by < devices]
    return lax.ppermute(array, axis, pairs)


def apply_blocks(inverse, vector):
    count = vector.shape[0]
    blocks = inverse.shape[0]
    shaped = vector.astype(jnp.bfloat16).reshape(count, blocks, 128)
    result = jnp.einsum("bij,rbj->rbi", inverse, shaped, preferred_element_type=jnp.float32)
    return result.reshape(count, blocks * 128)


def section_solve(g_flat, rhs_sep, apply_leaf, sep_blocks, row_map, weights):
    count = g_flat.shape[0]
    plane_cells = g_flat.shape[1] // PLANES
    sep_rows = rhs_sep.shape[1]
    leaves = lax.axis_size("nd")
    y_all = apply_leaf(g_flat)
    y_edge = y_all.reshape(count, PLANES, plane_cells)[:, :, :EDGE].reshape(count, PLANES * EDGE)
    contrib = y_edge * weights[None]
    spread = jnp.zeros((count, sep_rows * leaves), jnp.float32).at[:, row_map].add(contrib)
    summed = lax.psum_scatter(spread, "nd", scatter_dimension=1, tiled=True)
    sep_value = apply_blocks(sep_blocks, rhs_sep - summed)
    whole = lax.all_gather(sep_value, "nd", axis=1, tiled=True)
    picked = whole[:, row_map]
    correction = (picked * weights[None]).reshape(count, PLANES, EDGE)
    held = g_flat.reshape(count, PLANES, plane_cells).at[:, :, :EDGE].add(-correction)
    x_leaf = apply_leaf(held.reshape(count, -1))
    return (x_leaf, sep_value)


def shards(f_int, f_sep, leaf_inverse, sep_inverse, sep_map, couple, trace_coef):
    rhs_int = f_int[0]
    rhs_sep = f_sep[0]
    leaf_blocks = leaf_inverse[0]
    sep_blocks = sep_inverse[0]
    row_map = sep_map[0]
    weights = couple[0]
    coef = trace_coef[0]
    columns = rhs_int.shape[0]
    leaf_rows = rhs_int.shape[1]
    plane_cells = leaf_rows // PLANES
    sections = lax.axis_size("sweep")

    def apply_leaf(vector):
        return apply_blocks(leaf_blocks, vector)

    def whole_step(step, carry):
        trace, x_leaf, sep_value = carry
        grid = rhs_int.reshape(columns, PLANES, plane_cells).at[:, 0, :].add(-coef[None] * trace)
        x_leaf, sep_value = section_solve(
            grid.reshape(columns, leaf_rows), rhs_sep, apply_leaf, sep_blocks, row_map, weights
        )
        last = x_leaf[:, leaf_rows - plane_cells :]
        trace = passed_along(last, "sweep", 1)
        return (trace, x_leaf, sep_value)

    start = (
        jnp.zeros((columns, plane_cells), jnp.float32),
        jnp.zeros_like(rhs_int),
        jnp.zeros_like(rhs_sep),
    )
    final = lax.fori_loop(0, sections, whole_step, start)
    return (final[1][None], final[2][None])


def solution(mesh):
    placed = (
        P("sweep", None, "nd"),
        P("sweep", None, "nd"),
        P("sweep", "nd", None, None),
        P("sweep", "nd", None, None),
        P("sweep", "nd"),
        P("sweep", "nd"),
        P("sweep", "nd"),
    )
    return jax.shard_map(
        shards,
        mesh=mesh,
        in_specs=placed,
        out_specs=(P("sweep", None, "nd"), P("sweep", None, "nd")),
        check_vma=False,
    )
```

profile of v0, /device:TPU:3, one launch (start us, length us, event | category | flops | bytes accessed | tf_op | source)
XLA Modules:
  0.0 888.1 jit_solution(6188719416456780348)
XLA Ops:
  9.6 872.0 %while.19 = (s32[]{:T(128)}, f32[4,2048]{1,0:T(4,128)S(1)}, f32[4,32768]{1,0:T(4,128)}, f32[4,1024]{1,0:T(4,128)}, f32[1,4,32768]{2,1,0:T(4,128)}, /*index=5*/f3...) while((s32[]{:T(128)}, f32[4,2048]{1,0:T(4,128)S(1)}, ...), condition=%wide.region_3.4_spmd, body=%wide.region_0.3_spmd.sunk | while | flops 68493312 | bytes 33931604 | solution.py:74
  12.1 7.8 convolution_bitcast_fusion.6
  20.5 13.6 %scatter_custom_fusion.5 = f32[4,8192]{0,1:T(8,128)} fusion(s32[2048]{0:T(1024)S(1)} %bitcast.99, f32[2048,4]{1,0:T(8,128)S(1)} %copy.59, f32[]{:T(128)} %constant.96.clone.1..sunk), kind=kCustom, calls=%fused_computation.3.clone.1 | custom fusion | flops 8192 | bytes 131076 | tf_op jit(solution)/shard_map/while/body/eval_jaxpr/scatter-add | solution.py:32
  34.2 89.3 %reduce-scatter.2.cloned.1.call-done = f32[4,1024]{0,1:T(8,128)} async-done(((f32[4,8192]{0,1:T(8,128)}), f32[4,1024]{0,1:T(8,128)}) %reduce-scatter.2.cloned.1.call-update) | async-done | bytes 16400 | tf_op jit(solution)/shard_map/while/body/eval_jaxpr/reduce_scatter | solution.py:33
  125.1 81.9 %all_gather.8 = f32[4,8192]{0,1:T(8,128)} all-gather(f32[4,1024]{0,1:T(8,128)S(1)} %copy.60), channel_id=1, replica_groups=mesh['sweep'=4,'nd'=8] {'nd'}, dimensions={1}, use_global_device_ids=true | all-gather | bytes 147456 | tf_op jit(solution)/shard_map/while/body/eval_jaxpr/all_gather | solution.py:35
  207.1 7.6 gather_fusion
  215.2 7.8 convolution_bitcast_fusion.8
  230.0 7.8 convolution_bitcast_fusion.6
  238.4 13.6 %scatter_custom_fusion.5 = f32[4,8192]{0,1:T(8,128)} fusion(s32[2048]{0:T(1024)S(1)} %bitcast.99, f32[2048,4]{1,0:T(8,128)S(1)} %copy.59, f32[]{:T(128)} %constant.96.clone.1..sunk), kind=kCustom, calls=%fused_computation.3.clone.1 | custom fusion | flops 8192 | bytes 131076 | tf_op jit(solution)/shard_map/while/body/eval_jaxpr/scatter-add | solution.py:32
  252.1 89.6 %reduce-scatter.2.cloned.1.call-done = f32[4,1024]{0,1:T(8,128)} async-done(((f32[4,8192]{0,1:T(8,128)}), f32[4,1024]{0,1:T(8,128)}) %reduce-scatter.2.cloned.1.call-update) | async-done | bytes 16400 | tf_op jit(solution)/shard_map/while/body/eval_jaxpr/reduce_scatter | solution.py:33
  343.2 81.9 %all_gather.8 = f32[4,8192]{0,1:T(8,128)} all-gather(f32[4,1024]{0,1:T(8,128)S(1)} %copy.60), channel_id=1, replica_groups=mesh['sweep'=4,'nd'=8] {'nd'}, dimensions={1}, use_global_device_ids=true | all-gather | bytes 147456 | tf_op jit(solution)/shard_map/while/body/eval_jaxpr/all_gather | solution.py:35
  433.4 7.8 convolution_bitcast_fusion.8
  448.1 7.8 convolution_bitcast_fusion.6
  456.5 13.6 %scatter_custom_fusion.5 = f32[4,8192]{0,1:T(8,128)} fusion(s32[2048]{0:T(1024)S(1)} %bitcast.99, f32[2048,4]{1,0:T(8,128)S(1)} %copy.59, f32[]{:T(128)} %constant.96.clone.1..sunk), kind=kCustom, calls=%fused_computation.3.clone.1 | custom fusion | flops 8192 | bytes 131076 | tf_op jit(solution)/shard_map/while/body/eval_jaxpr/scatter-add | solution.py:32
  470.2 89.4 %reduce-scatter.2.cloned.1.call-done = f32[4,1024]{0,1:T(8,128)} async-done(((f32[4,8192]{0,1:T(8,128)}), f32[4,1024]{0,1:T(8,128)}) %reduce-scatter.2.cloned.1.call-update) | async-done | bytes 16400 | tf_op jit(solution)/shard_map/while/body/eval_jaxpr/reduce_scatter | solution.py:33
  561.2 82.3 %all_gather.8 = f32[4,8192]{0,1:T(8,128)} all-gather(f32[4,1024]{0,1:T(8,128)S(1)} %copy.60), channel_id=1, replica_groups=mesh['sweep'=4,'nd'=8] {'nd'}, dimensions={1}, use_global_device_ids=true | all-gather | bytes 147456 | tf_op jit(solution)/shard_map/while/body/eval_jaxpr/all_gather | solution.py:35
  643.4 7.6 gather_fusion
  651.6 7.8 convolution_bitcast_fusion.8
  666.1 7.8 convolution_bitcast_fusion.6
  674.4 13.6 %scatter_custom_fusion.5 = f32[4,8192]{0,1:T(8,128)} fusion(s32[2048]{0:T(1024)S(1)} %bitcast.99, f32[2048,4]{1,0:T(8,128)S(1)} %copy.59, f32[]{:T(128)} %constant.96.clone.1..sunk), kind=kCustom, calls=%fused_computation.3.clone.1 | custom fusion | flops 8192 | bytes 131076 | tf_op jit(solution)/shard_map/while/body/eval_jaxpr/scatter-add | solution.py:32
  688.1 89.4 %reduce-scatter.2.cloned.1.call-done = f32[4,1024]{0,1:T(8,128)} async-done(((f32[4,8192]{0,1:T(8,128)}), f32[4,1024]{0,1:T(8,128)}) %reduce-scatter.2.cloned.1.call-update) | async-done | bytes 16400 | tf_op jit(solution)/shard_map/while/body/eval_jaxpr/reduce_scatter | solution.py:33
  779.1 82.3 %all_gather.8 = f32[4,8192]{0,1:T(8,128)} all-gather(f32[4,1024]{0,1:T(8,128)S(1)} %copy.60), channel_id=1, replica_groups=mesh['sweep'=4,'nd'=8] {'nd'}, dimensions={1}, use_global_device_ids=true | all-gather | bytes 147456 | tf_op jit(solution)/shard_map/while/body/eval_jaxpr/all_gather | solution.py:35
  861.4 7.6 gather_fusion
  869.6 7.8 convolution_bitcast_fusion.8
  (139 shorter events, 47.9 us)
Async XLA Ops:
  9.6 113.9 %reduce-scatter.2.cloned.1.call-start = ((), (), s32[]{:S(2)}) async-start(), calls=%async_computation.1 | async-start | bytes 4718592 | tf_op jit(solution)/shard_map/while/body/eval_jaxpr/reduce_scatter | solution.py:33
  12.1 8.0 copy-start.1
  20.5 104.1 %copy-start = (bf16[8,128,128]{2,1,0:T(8,128)(2,1)S(1)}, bf16[8,128,128]{2,1,0:T(8,128)(2,1)}, u32[]{:S(2)}) copy-start(bf16[8,128,128]{2,1,0:T(8,128)(2,1)} %get-tuple-element.342) | copy-start | bytes 786436 | tf_op jit(solution)/shard_map/while
  124.9 98.2 %copy-start.2 = (f32[4,1024]{1,0:T(4,128)}, f32[4,1024]{1,0:T(4,128)S(1)}, u32[]{:S(2)}) copy-start(f32[4,1024]{1,0:T(4,128)S(1)} %convolution_bitcast_fusion.7) | copy-start | bytes 49156 | tf_op jit(solution)/shard_map/while
  223.0 4.5 copy-start.3
  223.1 4.5 collective-permute-start
  227.6 114.1 %reduce-scatter.2.cloned.1.call-start = ((), (), s32[]{:S(2)}) async-start(), calls=%async_computation.1 | async-start | bytes 4718592 | tf_op jit(solution)/shard_map/while/body/eval_jaxpr/reduce_scatter | solution.py:33
  230.0 8.0 copy-start.1
  238.4 104.3 %copy-start = (bf16[8,128,128]{2,1,0:T(8,128)(2,1)S(1)}, bf16[8,128,128]{2,1,0:T(8,128)(2,1)}, u32[]{:S(2)}) copy-start(bf16[8,128,128]{2,1,0:T(8,128)(2,1)} %get-tuple-element.342) | copy-start | bytes 786436 | tf_op jit(solution)/shard_map/while
  343.0 98.2 %copy-start.2 = (f32[4,1024]{1,0:T(4,128)}, f32[4,1024]{1,0:T(4,128)S(1)}, u32[]{:S(2)}) copy-start(f32[4,1024]{1,0:T(4,128)S(1)} %convolution_bitcast_fusion.7) | copy-start | bytes 49156 | tf_op jit(solution)/shard_map/while
  441.1 4.5 copy-start.3
  441.2 4.5 collective-permute-start
  445.7 113.9 %reduce-scatter.2.cloned.1.call-start = ((), (), s32[]{:S(2)}) async-start(), calls=%async_computation.1 | async-start | bytes 4718592 | tf_op jit(solution)/shard_map/while/body/eval_jaxpr/reduce_scatter | solution.py:33
  448.1 8.0 copy-start.1
  456.5 104.2 %copy-start = (bf16[8,128,128]{2,1,0:T(8,128)(2,1)S(1)}, bf16[8,128,128]{2,1,0:T(8,128)(2,1)}, u32[]{:S(2)}) copy-start(bf16[8,128,128]{2,1,0:T(8,128)(2,1)} %get-tuple-element.342) | copy-start | bytes 786436 | tf_op jit(solution)/shard_map/while
  560.9 98.5 %copy-start.2 = (f32[4,1024]{1,0:T(4,128)}, f32[4,1024]{1,0:T(4,128)S(1)}, u32[]{:S(2)}) copy-start(f32[4,1024]{1,0:T(4,128)S(1)} %convolution_bitcast_fusion.7) | copy-start | bytes 49156 | tf_op jit(solution)/shard_map/while
  659.4 4.2 copy-start.3
  659.4 4.2 collective-permute-start
  663.6 113.9 %reduce-scatter.2.cloned.1.call-start = ((), (), s32[]{:S(2)}) async-start(), calls=%async_computation.1 | async-start | bytes 4718592 | tf_op jit(solution)/shard_map/while/body/eval_jaxpr/reduce_scatter | solution.py:33
  666.1 8.0 copy-start.1
  674.4 104.2 %copy-start = (bf16[8,128,128]{2,1,0:T(8,128)(2,1)S(1)}, bf16[8,128,128]{2,1,0:T(8,128)(2,1)}, u32[]{:S(2)}) copy-start(bf16[8,128,128]{2,1,0:T(8,128)(2,1)} %get-tuple-element.342) | copy-start | bytes 786436 | tf_op jit(solution)/shard_map/while
  778.9 98.5 %copy-start.2 = (f32[4,1024]{1,0:T(4,128)}, f32[4,1024]{1,0:T(4,128)S(1)}, u32[]{:S(2)}) copy-start(f32[4,1024]{1,0:T(4,128)S(1)} %convolution_bitcast_fusion.7) | copy-start | bytes 49156 | tf_op jit(solution)/shard_map/while
  877.3 4.2 copy-start.3
  877.4 4.2 collective-permute-start
Sparse Core Ops, SparseCore 0:
  34.3 89.1 reduce-scatter.1
  252.2 89.3 reduce-scatter.1
  470.3 89.2 reduce-scatter.1
  688.2 89.2 reduce-scatter.1
where the time goes:
time: 892 us; the launch traced here: 888 us
  waiting for transfers between devices  370 us (41%)
  blocking collectives  328 us (37%)
  matrix products  63.3 us (7%)
  other arithmetic  62.9 us (7%)
  local copies, waits for them, and re-layouts  44 us (5%)
  between operations  13.7 us (2%)
    reduce_scatter x4, waiting for transfers between devices, section_solve(): summed = lax.psum_scatter(spread, 'nd', scatter_dimension=1, tiled=True)  358 us
    all_gather x4, blocking collectives, section_solve(): whole = lax.all_gather(sep_value, 'nd', axis=1, tiled=True)  328 us
    dot_general x12, matrix products, apply_blocks(): jnp.einsum('bij,rbj->rbi', inverse, shaped, preferred_element_type=jnp.fl...  63.3 us
    scatter-add x4, other arithmetic, section_solve(): jnp.zeros((count, sep_rows * leaves), jnp.float32).at[:, row_map]  54.5 us
    gather x8, local copies, waits for them, and re-layouts, section_solve(): picked = whole[:, row_map]  31.9 us
  transfers between devices with their start and end apart: 8, of which 8 were waited for; matrix products, arithmetic and copies ran while one was open for 0% of the time, Pallas kernels for 0%

commit v1 on v0

v1 whole, which is shorter than its diff:
```python
import functools

import jax
import jax.numpy as jnp
from jax import lax
from jax.experimental import pallas as pl
from jax.experimental.pallas import tpu as pltpu
from jax.sharding import PartitionSpec as P

MESH = pl.DeviceIdType.MESH
PLANES = 16
B = 128
F32 = jnp.float32
BF16 = jnp.bfloat16


def dot_nt(a, b):
    return lax.dot_general(a, b, (((1,), (1,)), ((), ())), preferred_element_type=F32)


def dot_nn(a, b):
    return lax.dot_general(a, b, (((1,), (0,)), ((), ())), preferred_element_type=F32)


def split(x):
    high = x.astype(BF16)
    return high, (x - high.astype(F32)).astype(BF16)


def one_hot_rows(low, rows=B):
    shape = (rows, low.shape[1])
    return jnp.where(lax.broadcasted_iota(jnp.int32, shape, 0) == low, 1.0, 0.0).astype(BF16)


def kernel(S, n, leaf_hbm, f_hbm, fsep, sepinv, smap, couple, coef, xint, xsep,
           leaf, f, onehot, scat, maps, own0, own15, base_out, base_in, v_in, pick_out, pick_in,
           xall, l240_out, l240_in, aux_out, aux_in, t_out, t_in, g0,
           load_sem, map_s, map_r, base_s, base_r, v_s, v_r, pick_s, pick_r, x_s, x_r, fwd_s, fwd_r):
    columns = f.shape[1]
    plane = f.shape[2] // PLANES
    per = plane // B
    nh = fsep.shape[2] // B
    total = n * nh
    s = lax.axis_index("sweep")
    me = lax.axis_index("nd")
    after = lax.rem(s + 1, S)
    before = lax.rem(s + S - 1, S)
    first = s == 0
    later = s > 0
    feeds = s < S - 1

    loads = [
        pltpu.make_async_copy(f_hbm, f, load_sem.at[0]),
        pltpu.make_async_copy(leaf_hbm.at[:, 0:1], leaf.at[:, 0:1], load_sem.at[1]),
        pltpu.make_async_copy(leaf_hbm.at[PLANES - 1:PLANES, 1:per], leaf.at[PLANES - 1:PLANES, 1:per], load_sem.at[2]),
        pltpu.make_async_copy(leaf_hbm.at[0:PLANES - 1, 1:per], leaf.at[0:PLANES - 1, 1:per], load_sem.at[3]),
    ]
    for load in loads:
        load.start()

    barrier = pltpu.get_barrier_semaphore()
    for k in range(1, n):
        pl.semaphore_signal(barrier, inc=1, device_id={"sweep": s, "nd": lax.rem(me + k, n)}, device_id_type=MESH)
    for k in range(n):
        other = lax.rem(me + k, n)
        pl.semaphore_signal(barrier, inc=1, device_id={"sweep": after, "nd": other}, device_id_type=MESH)
        pl.semaphore_signal(barrier, inc=1, device_id={"sweep": before, "nd": other}, device_id_type=MESH)

    def to(src, dst, send, recv, sweep, nd):
        return pltpu.make_async_remote_copy(
            src_ref=src, dst_ref=dst, send_sem=send, recv_sem=recv,
            device_id={"sweep": sweep, "nd": nd}, device_id_type=MESH)

    def map_copy(k):
        return to(maps.at[0], maps.at[k], map_s.at[k], map_r.at[k], s, lax.rem(me + k, n))

    def base_copy(k):
        other = lax.rem(me + k, n)
        return to(base_out.at[other], base_in.at[k], base_s.at[k], base_r.at[k], s, other)

    def v_copy(k):
        return to(v_in.at[0], v_in.at[k], v_s.at[k], v_r.at[k], s, lax.rem(me + k, n))

    def pick_copy(k):
        return to(pick_out.at[k], pick_in.at[k], pick_s.at[k], pick_r.at[k], after, lax.rem(me + n - k, n))

    def x_copy(k):
        return to(xall.at[me], xall.at[me], x_s.at[k], x_r.at[k], s, lax.rem(me + k, n))

    l240_copy = to(l240_out, l240_in, fwd_s.at[0], fwd_r.at[0], after, me)
    aux_copy = to(aux_out, aux_in, fwd_s.at[1], fwd_r.at[1], after, me)
    t_copy = to(t_out, t_in, fwd_s.at[2], fwd_r.at[2], after, me)

    maps[0, 0:1, :] = smap[0:1, 0:B]
    maps[0, 1:2, :] = smap[0:1, (PLANES - 1) * B:PLANES * B]
    row_map = smap[0:1, :]
    low = jnp.bitwise_and(row_map, B - 1)
    high = jnp.right_shift(row_map, 7)
    hot = one_hot_rows(low)
    onehot[0:B, :] = hot
    onehot[B:2 * B, :] = hot
    for h in range(nh):
        scat[:, h * B:(h + 1) * B] = sepinv[0, h]

    pl.semaphore_wait(barrier, 3 * n - 1)
    for k in range(1, n):
        map_copy(k).start()

    loads[0].wait()
    loads[1].wait()
    aux_out[0:columns, :] = f[0, :, (PLANES - 1) * plane:(PLANES - 1) * plane + B]
    aux_out[columns:columns + 1, :] = couple[0:1, (PLANES - 1) * B:PLANES * B]
    l240_out[...] = leaf[PLANES - 1, 0].astype(F32)

    @pl.when(feeds)
    def _():
        l240_copy.start()
        aux_copy.start()

    parts = [jnp.zeros((columns, B), F32)]
    for p in range(1, PLANES):
        g = f[0, :, p * plane:p * plane + B].astype(BF16)
        parts.append(dot_nt(g, leaf[p, 0]) * couple[0:1, p * B:(p + 1) * B])
    vals = jnp.concatenate(parts, axis=1)
    v_high, v_low = split(vals)
    v_high, v_low = v_high.astype(F32), v_low.astype(F32)
    is_high = lax.broadcasted_iota(jnp.int32, (total, PLANES * B), 0) == high
    rows = []
    for piece in (v_high, v_low):
        for r in range(columns):
            rows.append(jnp.where(is_high, piece[r:r + 1, :], 0.0).astype(BF16))
    spread = dot_nt(jnp.concatenate(rows, axis=0), onehot[0:B, :])
    for r in range(columns):
        both = spread[r * total:(r + 1) * total] + spread[(columns + r) * total:(columns + r + 1) * total]
        base_out[:, r * nh:(r + 1) * nh, :] = both.reshape(n, nh, B)
    for k in range(1, n):
        base_copy(k).start()

    def send_v():
        y0 = dot_nt(g0[...].astype(BF16), leaf[0, 0])
        v_in[0] = y0 * couple[0:1, 0:B]
        for k in range(1, n):
            v_copy(k).start()

    @pl.when(first)
    def _():
        g0[...] = f[0, :, 0:B]
        send_v()

    loads[2].wait()
    for b in range(1, per):
        at = (PLANES - 1) * plane + b * B
        out = dot_nt(f[0, :, at:at + B].astype(BF16), leaf[PLANES - 1, b])
        xint[0, :, at:at + B] = out
        t_out[:, b * B:(b + 1) * B] = out
    t_out[:, 0:B] = jnp.zeros((columns, B), F32)

    @pl.when(feeds)
    def _():
        t_copy.start()

    for k in range(1, n):
        map_copy(k).wait_recv()
    map0 = jnp.concatenate([maps[k, 0:1, :] for k in range(n)], axis=1)
    map15 = jnp.concatenate([maps[k, 1:2, :] for k in range(n)], axis=1)
    own0[...] = one_hot_rows(jnp.bitwise_and(map0, B - 1))
    hot15 = one_hot_rows(jnp.bitwise_and(map15, B - 1))
    own15[0:B, :] = hot15
    own15[B:2 * B, :] = hot15
    near = lax.broadcasted_iota(jnp.int32, (nh, n * B), 0) + me * nh
    is0 = near == jnp.right_shift(map0, 7)
    is15 = near == jnp.right_shift(map15, 7)

    def bulk():
        loads[3].wait()

        def one_plane(p, carry):
            for b in range(1, per):
                at = pl.multiple_of(p * plane + b * B, B)
                xint[0, :, pl.ds(at, B)] = dot_nt(f[0, :, pl.ds(at, B)].astype(BF16), leaf[p, b])
            return carry

        lax.fori_loop(1, PLANES - 1, one_plane, 0)

    @pl.when(later)
    def _():
        bulk()
        t_copy.wait_recv()
        for b in range(1, per):
            cut = slice(b * B, (b + 1) * B)
            g = f[0, :, cut] - coef[0:1, cut] * t_in[:, cut]
            xint[0, :, cut] = dot_nt(g.astype(BF16), leaf[0, b])
        l240_copy.wait_recv()
        aux_copy.wait_recv()
        l240 = l240_in[...].astype(BF16)
        for k in range(n):
            pick_copy(k).wait_recv()
        picked = pick_in[0]
        for k in range(1, n):
            picked = picked + pick_in[k]
        h = aux_in[0:columns, :] - aux_in[columns:columns + 1, :] * picked
        t = dot_nt(h.astype(BF16), l240)
        g0[...] = f[0, :, 0:B] - coef[0:1, 0:B] * t
        send_v()

    sres = jnp.concatenate(
        [fsep[0, r:r + 1, h * B:(h + 1) * B] for r in range(columns) for h in range(nh)], axis=0)
    sres = sres - base_out[me]
    for k in range(1, n):
        base_copy(k).wait_recv()
        sres = sres - base_in[k]
    for k in range(1, n):
        v_copy(k).wait_recv()
    v = jnp.concatenate([v_in[k] for k in range(n)], axis=1)
    v_high, v_low = split(v)
    rows = []
    for piece in (v_high.astype(F32), v_low.astype(F32)):
        for r in range(columns):
            rows.append(jnp.where(is0, piece[r:r + 1, :], 0.0))
    spread = dot_nt(jnp.concatenate(rows, axis=0).astype(BF16), own0[...])
    many = columns * nh
    sres = sres - (spread[0:many] + spread[many:2 * many])
    which = lax.rem(lax.broadcasted_iota(jnp.int32, (many, B), 0), nh)
    wide = jnp.concatenate([jnp.where(which == h, sres, 0.0) for h in range(nh)], axis=1).astype(BF16)
    x = dot_nt(wide, scat[...])
    xall[me] = x
    x_high, x_low = split(x)
    found = dot_nn(jnp.concatenate([x_high, x_low], axis=1), own15[...])
    for r in range(columns):
        line = jnp.sum(jnp.where(is15, found[r * nh:(r + 1) * nh], 0.0), axis=0, keepdims=True)
        for k in range(n):
            pick_out[k, r:r + 1, :] = line[:, k * B:(k + 1) * B]

    @pl.when(feeds)
    def _():
        for k in range(n):
            pick_copy(k).start()

    for k in range(1, n):
        x_copy(k).start()
    for r in range(columns):
        for h in range(nh):
            xsep[0, r:r + 1, h * B:(h + 1) * B] = x[r * nh + h:r * nh + h + 1, :]

    @pl.when(first)
    def _():
        bulk()
        for b in range(1, per):
            cut = slice(b * B, (b + 1) * B)
            xint[0, :, cut] = dot_nt(f[0, :, cut].astype(BF16), leaf[0, b])

    for k in range(1, n):
        x_copy(k).wait_recv()
    stacked = jnp.concatenate(
        [xall[:, r * nh:(r + 1) * nh, :].reshape(total, B) for r in range(columns)], axis=0)
    x_high, x_low = split(stacked)
    stacked = jnp.concatenate([x_high, x_low], axis=1)
    wide = 4 * B
    for c in range(PLANES * B // wide):
        cut = slice(c * wide, (c + 1) * wide)
        found = dot_nn(stacked, onehot[:, cut])
        mask = lax.broadcasted_iota(jnp.int32, (total, wide), 0) == high[:, cut]
        lines = [
            jnp.sum(jnp.where(mask, found[r * total:(r + 1) * total], 0.0), axis=0, keepdims=True)
            for r in range(columns)]
        fix = jnp.concatenate(lines, axis=0) * couple[0:1, cut]
        for q in range(wide // B):
            p = c * (wide // B) + q
            at = p * plane
            g = g0[...] if p == 0 else f[0, :, at:at + B]
            h = g - fix[:, q * B:(q + 1) * B]
            xint[0, :, at:at + B] = dot_nt(h.astype(BF16), leaf[p, 0])

    for k in range(1, n):
        map_copy(k).wait_send()
        base_copy(k).wait_send()
        v_copy(k).wait_send()
        x_copy(k).wait_send()

    @pl.when(feeds)
    def _():
        l240_copy.wait_send()
        aux_copy.wait_send()
        t_copy.wait_send()
        for k in range(n):
            pick_copy(k).wait_send()


def solution(mesh):
    S, n = mesh.shape["sweep"], mesh.shape["nd"]

    def shards(f_int, f_sep, leaf_inverse, sep_inverse, sep_map, couple, trace_coef):
        columns, leaf_rows = f_int.shape[1], f_int.shape[2]
        plane = leaf_rows // PLANES
        per = plane // B
        sep_rows = f_sep.shape[2]
        nh = sep_rows // B
        blocks = leaf_inverse.reshape(PLANES, per, B, B)
        vmem = pl.BlockSpec(memory_space=pltpu.VMEM)
        hbm = pl.BlockSpec(memory_space=pl.ANY)
        dma = pltpu.SemaphoreType.DMA
        x_int, x_sep = pl.pallas_call(
            functools.partial(kernel, S, n),
            out_shape=(jax.ShapeDtypeStruct(f_int.shape, F32), jax.ShapeDtypeStruct(f_sep.shape, F32)),
            in_specs=[hbm, hbm] + [vmem] * 5,
            out_specs=(vmem, vmem),
            scratch_shapes=[
                pltpu.VMEM((PLANES, per, B, B), BF16),
                pltpu.VMEM((1, columns, leaf_rows), F32),
                pltpu.VMEM((2 * B, PLANES * B), BF16),
                pltpu.VMEM((B, sep_rows), BF16),
                pltpu.VMEM((n, 2, B), jnp.int32),
                pltpu.VMEM((B, n * B), BF16),
                pltpu.VMEM((2 * B, n * B), BF16),
                pltpu.VMEM((n, columns * nh, B), F32),
                pltpu.VMEM((n, columns * nh, B), F32),
                pltpu.VMEM((n, columns, B), F32),
                pltpu.VMEM((n, columns, B), F32),
                pltpu.VMEM((n, columns, B), F32),
                pltpu.VMEM((n, columns * nh, B), F32),
                pltpu.VMEM((B, B), F32),
                pltpu.VMEM((B, B), F32),
                pltpu.VMEM((8, B), F32),
                pltpu.VMEM((8, B), F32),
                pltpu.VMEM((columns, plane), F32),
                pltpu.VMEM((columns, plane), F32),
                pltpu.VMEM((columns, B), F32),
                dma((4,)),
            ] + [dma((n,))] * 10 + [dma((3,))] * 2,
            compiler_params=pltpu.CompilerParams(
                collective_id=0, has_side_effects=True, vmem_limit_bytes=48 * 1024 * 1024),
        )(blocks, f_int, f_sep, sep_inverse, sep_map, couple, trace_coef)
        return x_int, x_sep

    placed = (
        P("sweep", None, "nd"),
        P("sweep", None, "nd"),
        P("sweep", "nd", None, None),
        P("sweep", "nd", None, None),
        P("sweep", "nd"),
        P("sweep", "nd"),
        P("sweep", "nd"),
    )
    return jax.shard_map(
        shards,
        mesh=mesh,
        in_specs=placed,
        out_specs=(P("sweep", None, "nd"), P("sweep", None, "nd")),
        check_vma=False,
    )
```

time: 892 us -> 49.8 us (0.06)
  waiting for transfers between devices: 370 us -> 0 us
  blocking collectives: 328 us -> 0 us
  matrix products: 63.3 us -> 0 us
  other arithmetic: 62.9 us -> 0 us
  Pallas kernels: 0 us -> 42.5 us
  local copies, waits for them, and re-layouts: 44 us -> 6.19 us
  between operations: 13.7 us -> 0.65 us
    reduce_scatter x4 -> x0, waiting for transfers between devices: 358 us -> none  [section_solve(): summed = lax.psum_scatter(spread, 'nd', scatter_dimension=1, tiled=True)]
    all_gather x4 -> x0, blocking collectives: 328 us -> none  [section_solve(): whole = lax.all_gather(sep_value, 'nd', axis=1, tiled=True)]
    dot_general x12 -> x0, matrix products: 63.3 us -> none  [apply_blocks(): jnp.einsum('bij,rbj->rbi', inverse, shaped, preferred_element_type=jnp.fl...]
    scatter-add x8 -> x0, other arithmetic: 54.6 us -> none  [the longest x4 54.5 us: section_solve(): jnp.zeros((count, sep_rows * leaves), jnp.float32).at[:, row_map]]
    pallas_call x0 -> x1, Pallas kernels: none -> 42.5 us  [shards(): pl.pallas_call(functools.partial(kernel, S, n), out_shape=(jax.ShapeDtype...]
    gather x8 -> x0, local copies, waits for them, and re-layouts: 31.9 us -> none  [section_solve(): picked = whole[:, row_map]]
    ppermute x4 -> x0, waiting for transfers between devices: 12.1 us -> none  [passed_along(): return lax.ppermute(array, axis, pairs)]
  transfers between devices with their start and end apart: 8 -> 0, of which waited for: 8 -> 0; matrix products, arithmetic and copies ran while one was open for 0% -> 0% of each run, Pallas kernels for 0% -> 0%
where the time goes in v1:
time: 49.8 us; the launch traced here: 49.3 us
  Pallas kernels  42.5 us (85%)
  local copies, waits for them, and re-layouts  6.19 us (12%)
  between operations  0.65 us (1%)
    pallas_call x1, Pallas kernels, shards(): pl.pallas_call(functools.partial(kernel, S, n), out_shape=(jax.ShapeDtype...  42.5 us
    unnamed x14, local copies, waits for them, and re-layouts  6.19 us

profile of v1, /device:TPU:3, one launch (start us, length us, event | category | flops | bytes accessed | tf_op | source)
XLA Modules:
  0.0 49.3 jit_solution(7414068240561188827)
XLA Ops:
  0.6 0.0 copy-start
  0.6 1.0 %copy-done = f32[1,4,32768]{2,1,0:T(4,128)S(1)} copy-done((f32[1,4,32768]{2,1,0:T(4,128)S(1)}, f32[1,4,32768]{2,1,0:T(4,128)}, u32[]{:S(2)}) %copy-start) | copy-done | bytes 524312
  1.7 0.0 copy-start.1
  1.7 0.9 %copy-done.1 = bf16[1,8,128,128]{3,2,1,0:T(8,128)(2,1)S(1)} copy-done((bf16[1,8,128,128]{3,2,1,0:T(8,128)(2,1)S(1)}, bf16[1,8,128,128]{3,2,1,0:T(8,128)(2,1)}, u32[]{:S(2)}) %copy-start.1) | copy-done | bytes 262168
  2.6 0.0 copy-start.2
  2.6 0.7 %copy-done.2 = f32[1,4,1024]{2,1,0:T(4,128)S(1)} copy-done((f32[1,4,1024]{2,1,0:T(4,128)S(1)}, f32[1,4,1024]{2,1,0:T(4,128)}, u32[]{:S(2)}) %copy-start.2) | copy-done | bytes 16408
  3.3 0.0 copy-start.3
  3.3 0.7 %copy-done.3 = s32[1,2048]{1,0:T(1,128)S(1)} copy-done((s32[1,2048]{1,0:T(1,128)S(1)}, s32[1,2048]{1,0:T(1,128)}, u32[]{:S(2)}) %copy-start.3) | copy-done | bytes 8216
  4.0 0.0 copy-start.4
  4.0 0.7 %copy-done.4 = f32[1,2048]{1,0:T(1,128)S(1)} copy-done((f32[1,2048]{1,0:T(1,128)S(1)}, f32[1,2048]{1,0:T(1,128)}, u32[]{:S(2)}) %copy-start.4) | copy-done | bytes 8216
  4.7 0.0 copy-start.5
  4.7 0.7 %copy-done.5 = f32[1,2048]{1,0:T(1,128)S(1)} copy-done((f32[1,2048]{1,0:T(1,128)S(1)}, f32[1,2048]{1,0:T(1,128)}, u32[]{:S(2)}) %copy-start.5) | copy-done | bytes 8216
  5.4 42.5 %shard_map.86 = (f32[1,4,32768]{2,1,0:T(4,128)S(1)}, f32[1,4,1024]{2,1,0:T(4,128)S(1)}) custom-call(bf16[16,16,128,128]{3,2,1,0:T(8,128)(2,1)} %bitcast.1, f32[1,4,32768]{2,1,0:T(4,128)S(1)} %copy-done, f32[1,4,1024]{2,1,0:T(4,128)S(1)} %copy-done.2, bf16[1,8,128,128]{3,2,1,0:T(8,128)(2,1)S(1)} %copy-done.1, s32[1,2048]{1,0:T(1,128)S(1)} %copy-done.3, ...), custom_call_target="tpu_custom_call" | custom-call | tf_op jit(solution)/shard_map/pallas_call | solution.py:302
  47.9 0.8 %copy.11 = f32[1,4,32768]{2,1,0:T(4,128)} copy(f32[1,4,32768]{2,1,0:T(4,128)S(1)} %get-tuple-element.4) | data formatting | bytes 1048576
  48.7 0.6 %copy.12 = f32[1,4,1024]{2,1,0:T(4,128)} copy(f32[1,4,1024]{2,1,0:T(4,128)S(1)} %get-tuple-element.5) | data formatting | bytes 32768
Async XLA Ops:
  0.6 1.0 %copy-start = (f32[1,4,32768]{2,1,0:T(4,128)S(1)}, f32[1,4,32768]{2,1,0:T(4,128)}, u32[]{:S(2)}) copy-start(f32[1,4,32768]{2,1,0:T(4,128)} %f_hbm.1) | copy-start | bytes 1572868
  1.7 0.9 %copy-start.1 = (bf16[1,8,128,128]{3,2,1,0:T(8,128)(2,1)S(1)}, bf16[1,8,128,128]{3,2,1,0:T(8,128)(2,1)}, u32[]{:S(2)}) copy-start(bf16[1,8,128,128]{3,2,1,0:T(8,128)(2,1)} %sepinv.1) | copy-start | bytes 786436
  2.6 0.7 %copy-start.2 = (f32[1,4,1024]{2,1,0:T(4,128)S(1)}, f32[1,4,1024]{2,1,0:T(4,128)}, u32[]{:S(2)}) copy-start(f32[1,4,1024]{2,1,0:T(4,128)} %fsep.1) | copy-start | bytes 49156
  3.3 0.7 %copy-start.3 = (s32[1,2048]{1,0:T(1,128)S(1)}, s32[1,2048]{1,0:T(1,128)}, u32[]{:S(2)}) copy-start(s32[1,2048]{1,0:T(1,128)} %smap.1) | copy-start | bytes 24580
  4.0 0.7 %copy-start.4 = (f32[1,2048]{1,0:T(1,128)S(1)}, f32[1,2048]{1,0:T(1,128)}, u32[]{:S(2)}) copy-start(f32[1,2048]{1,0:T(1,128)} %couple.1) | copy-start | bytes 24580
  4.7 0.7 %copy-start.5 = (f32[1,2048]{1,0:T(1,128)S(1)}, f32[1,2048]{1,0:T(1,128)}, u32[]{:S(2)}) copy-start(f32[1,2048]{1,0:T(1,128)} %coef.1) | copy-start | bytes 24580

commit v2 on v1

--- a/solution.py
+++ b/solution.py
@@ -32,10 +32,10 @@
     return jnp.where(lax.broadcasted_iota(jnp.int32, shape, 0) == low, 1.0, 0.0).astype(BF16)
 
 
-def kernel(S, n, leaf_hbm, f_hbm, fsep, sepinv, smap, couple, coef, xint, xsep,
-           leaf, f, onehot, scat, maps, own0, own15, base_out, base_in, v_in, pick_out, pick_in,
+def kernel(S, n, leaf_hbm, f_hbm, fsep_hbm, sepinv_hbm, smap_hbm, couple_hbm, coef_hbm, xint, xsep,
+           leaf, f, fsep, sepinv, smap, couple, coef, onehot, scat, own0, own15, base_out, base_in, v_in, pick_out, pick_in,
            xall, l240_out, l240_in, aux_out, aux_in, t_out, t_in, g0,
-           load_sem, map_s, map_r, base_s, base_r, v_s, v_r, pick_s, pick_r, x_s, x_r, fwd_s, fwd_r):
+           load_sem, base_s, base_r, v_s, v_r, pick_s, pick_r, x_s, x_r, fwd_s, fwd_r):
     columns = f.shape[1]
     plane = f.shape[2] // PLANES
     per = plane // B
@@ -50,8 +50,13 @@
     feeds = s < S - 1
 
     loads = [
+        pltpu.make_async_copy(smap_hbm, smap, load_sem.at[4]),
         pltpu.make_async_copy(f_hbm, f, load_sem.at[0]),
         pltpu.make_async_copy(leaf_hbm.at[:, 0:1], leaf.at[:, 0:1], load_sem.at[1]),
+        pltpu.make_async_copy(couple_hbm, couple, load_sem.at[5]),
+        pltpu.make_async_copy(sepinv_hbm, sepinv, load_sem.at[6]),
+        pltpu.make_async_copy(fsep_hbm, fsep, load_sem.at[7]),
+        pltpu.make_async_copy(coef_hbm, coef, load_sem.at[8]),
         pltpu.make_async_copy(leaf_hbm.at[PLANES - 1:PLANES, 1:per], leaf.at[PLANES - 1:PLANES, 1:per], load_sem.at[2]),
         pltpu.make_async_copy(leaf_hbm.at[0:PLANES - 1, 1:per], leaf.at[0:PLANES - 1, 1:per], load_sem.at[3]),
     ]
@@ -71,9 +76,6 @@
             src_ref=src, dst_ref=dst, send_sem=send, recv_sem=recv,
             device_id={"sweep": sweep, "nd": nd}, device_id_type=MESH)
 
-    def map_copy(k):
-        return to(maps.at[0], maps.at[k], map_s.at[k], map_r.at[k], s, lax.rem(me + k, n))
-
     def base_copy(k):
         other = lax.rem(me + k, n)
         return to(base_out.at[other], base_in.at[k], base_s.at[k], base_r.at[k], s, other)
@@ -91,36 +93,25 @@
     aux_copy = to(aux_out, aux_in, fwd_s.at[1], fwd_r.at[1], after, me)
     t_copy = to(t_out, t_in, fwd_s.at[2], fwd_r.at[2], after, me)
 
-    maps[0, 0:1, :] = smap[0:1, 0:B]
-    maps[0, 1:2, :] = smap[0:1, (PLANES - 1) * B:PLANES * B]
+    loads[0].wait()
     row_map = smap[0:1, :]
     low = jnp.bitwise_and(row_map, B - 1)
     high = jnp.right_shift(row_map, 7)
     hot = one_hot_rows(low)
     onehot[0:B, :] = hot
     onehot[B:2 * B, :] = hot
-    for h in range(nh):
-        scat[:, h * B:(h + 1) * B] = sepinv[0, h]
-
-    pl.semaphore_wait(barrier, 3 * n - 1)
-    for k in range(1, n):
-        map_copy(k).start()
-
-    loads[0].wait()
-    loads[1].wait()
+
+    for load in loads[1:4]:
+        load.wait()
     aux_out[0:columns, :] = f[0, :, (PLANES - 1) * plane:(PLANES - 1) * plane + B]
     aux_out[columns:columns + 1, :] = couple[0:1, (PLANES - 1) * B:PLANES * B]
     l240_out[...] = leaf[PLANES - 1, 0].astype(F32)
 
-    @pl.when(feeds)
-    def _():
-        l240_copy.start()
-        aux_copy.start()
-
-    parts = [jnp.zeros((columns, B), F32)]
-    for p in range(1, PLANES):
+    parts = []
+    for p in range(PLANES):
         g = f[0, :, p * plane:p * plane + B].astype(BF16)
         parts.append(dot_nt(g, leaf[p, 0]) * couple[0:1, p * B:(p + 1) * B])
+    parts[0] = jnp.where(first, parts[0], 0.0)
     vals = jnp.concatenate(parts, axis=1)
     v_high, v_low = split(vals)
     v_high, v_low = v_high.astype(F32), v_low.astype(F32)
@@ -133,8 +124,19 @@
     for r in range(columns):
         both = spread[r * total:(r + 1) * total] + spread[(columns + r) * total:(columns + r + 1) * total]
         base_out[:, r * nh:(r + 1) * nh, :] = both.reshape(n, nh, B)
+    many = columns * nh
+    ends = jnp.concatenate(
+        [smap[0:1, 0:B], smap[0:1, (PLANES - 1) * B:PLANES * B], jnp.zeros((6, B), jnp.int32)], axis=0).astype(F32)
+    for o in range(n):
+        base_out[o, many:many + 8, :] = ends
+    pl.semaphore_wait(barrier, 3 * n - 1)
     for k in range(1, n):
         base_copy(k).start()
+
+    @pl.when(feeds)
+    def _():
+        l240_copy.start()
+        aux_copy.start()
 
     def send_v():
         y0 = dot_nt(g0[...].astype(BF16), leaf[0, 0])
@@ -145,9 +147,14 @@
     @pl.when(first)
     def _():
         g0[...] = f[0, :, 0:B]
-        send_v()
-
-    loads[2].wait()
+        v_in[...] = jnp.zeros_like(v_in)
+
+    for load in loads[4:7]:
+        load.wait()
+    for h in range(nh):
+        scat[:, h * B:(h + 1) * B] = sepinv[0, h]
+
+    loads[7].wait()
     for b in range(1, per):
         at = (PLANES - 1) * plane + b * B
         out = dot_nt(f[0, :, at:at + B].astype(BF16), leaf[PLANES - 1, b])
@@ -159,10 +166,17 @@
     def _():
         t_copy.start()
 
-    for k in range(1, n):
-        map_copy(k).wait_recv()
-    map0 = jnp.concatenate([maps[k, 0:1, :] for k in range(n)], axis=1)
-    map15 = jnp.concatenate([maps[k, 1:2, :] for k in range(n)], axis=1)
+    sres = jnp.concatenate(
+        [fsep[0, r:r + 1, h * B:(h + 1) * B] for r in range(columns) for h in range(nh)], axis=0)
+    own = base_out[me]
+    sres = sres - own[0:many]
+    for k in range(1, n):
+        base_copy(k).wait_recv()
+        sres = sres - base_in[k, 0:many, :]
+    map0 = jnp.concatenate(
+        [own[many:many + 1]] + [base_in[k, many:many + 1, :] for k in range(1, n)], axis=1).astype(jnp.int32)
+    map15 = jnp.concatenate(
+        [own[many + 1:many + 2]] + [base_in[k, many + 1:many + 2, :] for k in range(1, n)], axis=1).astype(jnp.int32)
     own0[...] = one_hot_rows(jnp.bitwise_and(map0, B - 1))
     hot15 = one_hot_rows(jnp.bitwise_and(map15, B - 1))
     own15[0:B, :] = hot15
@@ -172,7 +186,7 @@
     is15 = near == jnp.right_shift(map15, 7)
 
     def bulk():
-        loads[3].wait()
+        loads[8].wait()
 
         def one_plane(p, carry):
             for b in range(1, per):
@@ -203,14 +217,11 @@
         g0[...] = f[0, :, 0:B] - coef[0:1, 0:B] * t
         send_v()
 
-    sres = jnp.concatenate(
-        [fsep[0, r:r + 1, h * B:(h + 1) * B] for r in range(columns) for h in range(nh)], axis=0)
-    sres = sres - base_out[me]
-    for k in range(1, n):
-        base_copy(k).wait_recv()
-        sres = sres - base_in[k]
-    for k in range(1, n):
-        v_copy(k).wait_recv()
+    @pl.when(later)
+    def _():
+        for k in range(1, n):
+            v_copy(k).wait_recv()
+
     v = jnp.concatenate([v_in[k] for k in range(n)], axis=1)
     v_high, v_low = split(v)
     rows = []
@@ -218,7 +229,6 @@
         for r in range(columns):
             rows.append(jnp.where(is0, piece[r:r + 1, :], 0.0))
     spread = dot_nt(jnp.concatenate(rows, axis=0).astype(BF16), own0[...])
-    many = columns * nh
     sres = sres - (spread[0:many] + spread[many:2 * many])
     which = lax.rem(lax.broadcasted_iota(jnp.int32, (many, B), 0), nh)
     wide = jnp.concatenate([jnp.where(which == h, sres, 0.0) for h in range(nh)], axis=1).astype(BF16)
@@ -272,10 +282,13 @@
             xint[0, :, at:at + B] = dot_nt(h.astype(BF16), leaf[p, 0])
 
     for k in range(1, n):
-        map_copy(k).wait_send()
         base_copy(k).wait_send()
-        v_copy(k).wait_send()
         x_copy(k).wait_send()
+
+    @pl.when(later)
+    def _():
+        for k in range(1, n):
+            v_copy(k).wait_send()
 
     @pl.when(feeds)
     def _():
@@ -297,23 +310,27 @@
         nh = sep_rows // B
         blocks = leaf_inverse.reshape(PLANES, per, B, B)
         vmem = pl.BlockSpec(memory_space=pltpu.VMEM)
-        hbm = pl.BlockSpec(memory_space=pl.ANY)
+        hbm = pl.BlockSpec(memory_space=pltpu.HBM)
         dma = pltpu.SemaphoreType.DMA
         x_int, x_sep = pl.pallas_call(
             functools.partial(kernel, S, n),
-            out_shape=(jax.ShapeDtypeStruct(f_int.shape, F32), jax.ShapeDtypeStruct(f_sep.shape, F32)),
-            in_specs=[hbm, hbm] + [vmem] * 5,
+            out_shape=(pltpu.VMEM(f_int.shape, F32), pltpu.VMEM(f_sep.shape, F32)),
+            in_specs=[hbm] * 7,
             out_specs=(vmem, vmem),
             scratch_shapes=[
                 pltpu.VMEM((PLANES, per, B, B), BF16),
                 pltpu.VMEM((1, columns, leaf_rows), F32),
+                pltpu.VMEM(f_sep.shape, F32),
+                pltpu.VMEM(sep_inverse.shape, BF16),
+                pltpu.VMEM(sep_map.shape, jnp.int32),
+                pltpu.VMEM(couple.shape, F32),
+                pltpu.VMEM(trace_coef.shape, F32),
                 pltpu.VMEM((2 * B, PLANES * B), BF16),
                 pltpu.VMEM((B, sep_rows), BF16),
-                pltpu.VMEM((n, 2, B), jnp.int32),
                 pltpu.VMEM((B, n * B), BF16),
                 pltpu.VMEM((2 * B, n * B), BF16),
-                pltpu.VMEM((n, columns * nh, B), F32),
-                pltpu.VMEM((n, columns * nh, B), F32),
+                pltpu.VMEM((n, columns * nh + 8, B), F32),
+                pltpu.VMEM((n, columns * nh + 8, B), F32),
                 pltpu.VMEM((n, columns, B), F32),
                 pltpu.VMEM((n, columns, B), F32),
                 pltpu.VMEM((n, columns, B), F32),
@@ -325,10 +342,10 @@
                 pltpu.VMEM((columns, plane), F32),
                 pltpu.VMEM((columns, plane), F32),
                 pltpu.VMEM((columns, B), F32),
-                dma((4,)),
-            ] + [dma((n,))] * 10 + [dma((3,))] * 2,
+                dma((9,)),
+            ] + [dma((n,))] * 8 + [dma((3,))] * 2,
             compiler_params=pltpu.CompilerParams(
-                collective_id=0, has_side_effects=True, vmem_limit_bytes=48 * 1024 * 1024),
+                collective_id=0, has_side_effects=True, vmem_limit_bytes=56 * 1024 * 1024),
         )(blocks, f_int, f_sep, sep_inverse, sep_map, couple, trace_coef)
         return x_int, x_sep
 

time: 49.8 us -> 44.4 us (0.89)
  local copies, waits for them, and re-layouts: 6.19 us -> 1.4 us
    unnamed x14 -> x2, local copies, waits for them, and re-layouts: 6.19 us -> 1.4 us
where the time goes in v2:
time: 44.4 us; the launch traced here: 44.2 us
  Pallas kernels  42.1 us (95%)
  local copies, waits for them, and re-layouts  1.4 us (3%)
  between operations  0.64 us (1%)
    pallas_call x1, Pallas kernels, shards(): pl.pallas_call(functools.partial(kernel, S, n), out_shape=(pltpu.VMEM(f_i...  42.1 us
    unnamed x2, local copies, waits for them, and re-layouts  1.4 us

profile of v2, /device:TPU:3, one launch (start us, length us, event | category | flops | bytes accessed | tf_op | source)
XLA Modules:
  0.0 44.2 jit_solution(28285189151491573)
XLA Ops:
  0.6 42.1 %shard_map.86 = (f32[1,4,32768]{2,1,0:T(4,128)S(1)}, f32[1,4,1024]{2,1,0:T(4,128)S(1)}) custom-call(bf16[16,16,128,128]{3,2,1,0:T(8,128)(2,1)} %bitcast.1, f32[1,4,32768]{2,1,0:T(4,128)} %f_hbm.1, f32[1,4,1024]{2,1,0:T(4,128)} %fsep_hbm.1, bf16[1,8,128,128]{3,2,1,0:T(8,128)(2,1)} %sepinv_hbm.1, s32[1,2048]{1,0:T(1,128)} %smap_hbm.1, f32[1,2048]{1,0:T(1,128)} %couple_hbm.1, ...), custom_call_target="tpu_custom_call" | custom-call | tf_op jit(solution)/shard_map/pallas_call | solution.py:315
  42.8 0.8 %copy.11 = f32[1,4,32768]{2,1,0:T(4,128)} copy(f32[1,4,32768]{2,1,0:T(4,128)S(1)} %get-tuple-element.2) | data formatting | bytes 1048576
  43.6 0.6 %copy.12 = f32[1,4,1024]{2,1,0:T(4,128)} copy(f32[1,4,1024]{2,1,0:T(4,128)S(1)} %get-tuple-element.3) | data formatting | bytes 32768

commit v3 on v2

--- a/solution.py
+++ b/solution.py
@@ -234,20 +234,27 @@
     wide = jnp.concatenate([jnp.where(which == h, sres, 0.0) for h in range(nh)], axis=1).astype(BF16)
     x = dot_nt(wide, scat[...])
     xall[me] = x
-    x_high, x_low = split(x)
-    found = dot_nn(jnp.concatenate([x_high, x_low], axis=1), own15[...])
-    for r in range(columns):
-        line = jnp.sum(jnp.where(is15, found[r * nh:(r + 1) * nh], 0.0), axis=0, keepdims=True)
-        for k in range(n):
-            pick_out[k, r:r + 1, :] = line[:, k * B:(k + 1) * B]
+
+    def send_x():
+        for k in range(1, n):
+            x_copy(k).start()
+
+    @pl.when(jnp.logical_not(feeds))
+    def _():
+        send_x()
 
     @pl.when(feeds)
     def _():
+        x_high, x_low = split(x)
+        found = dot_nn(jnp.concatenate([x_high, x_low], axis=1), own15[...])
+        for r in range(columns):
+            line = jnp.sum(jnp.where(is15, found[r * nh:(r + 1) * nh], 0.0), axis=0, keepdims=True)
+            for k in range(n):
+                pick_out[k, r:r + 1, :] = line[:, k * B:(k + 1) * B]
         for k in range(n):
             pick_copy(k).start()
-
-    for k in range(1, n):
-        x_copy(k).start()
+        send_x()
+
     for r in range(columns):
         for h in range(nh):
             xsep[0, r:r + 1, h * B:(h + 1) * B] = x[r * nh + h:r * nh + h + 1, :]

time: 44.4 us -> 44.3 us (level)
  no operation moved by 1% of the time
where the time goes in v3:
time: 44.3 us; the launch traced here: 44.1 us
  Pallas kernels  42 us (95%)
  local copies, waits for them, and re-layouts  1.4 us (3%)
  between operations  0.64 us (1%)
    pallas_call x1, Pallas kernels, shards(): pl.pallas_call(functools.partial(kernel, S, n), out_shape=(pltpu.VMEM(f_i...  42 us
    unnamed x2, local copies, waits for them, and re-layouts  1.4 us

profile of v3, /device:TPU:3, one launch (start us, length us, event | category | flops | bytes accessed | tf_op | source)
XLA Modules:
  0.0 44.1 jit_solution(4033559074552187563)
XLA Ops:
  0.6 42.0 %shard_map.86 = (f32[1,4,32768]{2,1,0:T(4,128)S(1)}, f32[1,4,1024]{2,1,0:T(4,128)S(1)}) custom-call(bf16[16,16,128,128]{3,2,1,0:T(8,128)(2,1)} %bitcast.1, f32[1,4,32768]{2,1,0:T(4,128)} %f_hbm.1, f32[1,4,1024]{2,1,0:T(4,128)} %fsep_hbm.1, bf16[1,8,128,128]{3,2,1,0:T(8,128)(2,1)} %sepinv_hbm.1, s32[1,2048]{1,0:T(1,128)} %smap_hbm.1, f32[1,2048]{1,0:T(1,128)} %couple_hbm.1, ...), custom_call_target="tpu_custom_call" | custom-call | tf_op jit(solution)/shard_map/pallas_call | solution.py:322
  42.7 0.8 %copy.11 = f32[1,4,32768]{2,1,0:T(4,128)} copy(f32[1,4,32768]{2,1,0:T(4,128)S(1)} %get-tuple-element.2) | data formatting | bytes 1048576
  43.5 0.6 %copy.12 = f32[1,4,1024]{2,1,0:T(4,128)} copy(f32[1,4,1024]{2,1,0:T(4,128)S(1)} %get-tuple-element.3) | data formatting | bytes 32768
